TPU v7x, 32 devices: a whole 2x2x4 slice. The times are simulated.
32 devices in a mesh: row: 16 (over z, y, x), col: 2 (over core).
Axes of the slice: x: 2, y: 2, z: 4, core: 2. Of those that a mesh axis runs over, the one named last changes fastest.
Arguments:
- panel: bfloat16 [16384, 4096], P('row', 'col'), may hold values from -60 to 60, as said below
- sketch: bfloat16 [4096, 256], P('col'), may hold values from -0.09375 to 0.09375
Outputs:
- basis: float32 [16384, 256], P(('row', 'col'))
- upper: float32 [256, 256], replicated
Inputs may be any that keep to these rules, and one draw needn't show every extreme that they name: `panel`: scaled expression values, real-valued, with scales that differ from cell to cell and from gene to gene.
All inputs are finite; a program needn't handle non-finite values.
Results may differ from a plain program's by a relative error of at most 0.0003.
Values sent between devices are 32-bit elements; how exact they have to be, the bound alone decides.
A program may use at most 64 MiB of HBM per device.

v0:
```python
import jax
import jax.numpy as jnp
from jax import lax
from jax.sharding import PartitionSpec as P


def local(panel, sketch):
    rows = panel.shape[0]
    share = rows // lax.axis_size("col")
    total_rows = rows * lax.axis_size("row")
    partial_value = jnp.dot(panel, sketch, preferred_element_type=jnp.float32)
    whole = lax.psum(partial_value, "col")
    local_gram = jnp.dot(whole.T, whole, precision=lax.Precision.HIGHEST)
    gram = lax.psum(local_gram, "row") / total_rows
    offset = lax.axis_index("col") * share
    block = lax.dynamic_slice_in_dim(whole, offset, share, 0)
    factor = jnp.linalg.cholesky(gram).T
    basis = jax.scipy.linalg.solve_triangular(factor.T, block.T, lower=True).T
    return (basis, factor)


def solution(mesh):
    return jax.shard_map(
        local,
        mesh=mesh,
        in_specs=(P("row", "col"), P("col", None)),
        out_specs=(P(("row", "col"), None), P()),
        check_vma=False,
    )
```

profile of v0, /device:TPU:0, one launch (start us, length us, event | category | flops | bytes accessed | tf_op | source)
XLA Modules:
  0.0 222.1 jit_solution(13599201051653722918)
XLA Ops:
  7.2 0.0 copy-start
  7.2 0.0 all-reduce.4.cloned.1.call-start
  7.2 1.2 copy-done
  8.4 4.5 %fusion.11 = f32[1024,256]{1,0:T(8,128)} fusion(bf16[1024,2048]{1,0:T(8,128)(2,1)} %param.2, bf16[2048,256]{1,0:T(8,128)(2,1)S(1)} %copy-done), kind=kOutput, calls=%fused_computation.33 | convolution fusion | flops 1073741824 | bytes 6291456 | tf_op jit(solution)/shard_map/dot_general | solution.py:11
  12.9 0.0 all-reduce.4.cloned.1.call-update
  12.9 0.0 all-reduce.6.cloned.1.call-start
  12.9 22.4 %all-reduce.4.cloned.1.call-done = f32[1024,256]{1,0:T(8,128)} async-done(((f32[1024,256]{1,0:T(8,128)}), f32[1024,256]{1,0:T(8,128)}) %all-reduce.4.cloned.1.call-update) | async-done | bytes 1048592 | tf_op jit(solution)/shard_map/psum | solution.py:12
  35.3 4.1 %fusion.12 = f32[256,256]{0,1:T(8,128)} fusion(f32[1024,256]{1,0:T(8,128)} %all-reduce.4.cloned.1.call-done), kind=kOutput, calls=%fused_computation.34 | convolution fusion | flops 805306368 | bytes 1310720 | tf_op jit(solution)/shard_map/dot_general | solution.py:13
  39.4 0.0 all-reduce.6.cloned.1.call-update
  39.5 1.1 dynamic-slice_bitcast_fusion
  40.6 109.3 %all-reduce.6.cloned.1.call-done = f32[256,256]{0,1:T(8,128)} async-done(((f32[256,256]{0,1:T(8,128)}), f32[256,256]{0,1:T(8,128)}) %all-reduce.6.cloned.1.call-update) | async-done | bytes 262160 | tf_op jit(solution)/shard_map/psum | solution.py:14
  149.9 1.0 broadcast_multiply_fusion
  150.9 0.1 copy.5
  151.0 1.0 fusion.2
  152.0 11.7 %cholesky.50 = f32[128,128]{1,0:T(8,128)S(1)} custom-call(f32[128,128]{1,0:T(8,128)S(1)} %cholesky.118), custom_call_target="Cholesky" | custom-call | tf_op jit(solution)/shard_map/jit(cholesky)/cholesky | solution.py:17
  163.8 9.8 %custom-call.15 = f32[1,128,128]{1,2,0:T(8,128)S(1)} custom-call(f32[1,128,128]{2,1,0:T(8,128)S(1)} %get-tuple-element.27), custom_call_target="InvertDiagBlocksLowerTriangular" | custom-call | tf_op jit(solution)/shard_map/jit(cholesky)/cholesky | solution.py:17
  173.6 0.2 constant_dynamic-update-slice_fusion
  173.8 0.3 convolution_subtract_fusion.1
  174.1 11.9 %cholesky.105 = f32[128,128]{1,0:T(8,128)S(1)} custom-call(f32[128,128]{1,0:T(8,128)S(1)} %convolution_subtract_fusion.1), custom_call_target="Cholesky" | custom-call | tf_op jit(solution)/shard_map/jit(cholesky)/cholesky | solution.py:17
  186.0 0.7 compare_reduce_fusion
  188.1 0.1 triangular_solve.57
  188.2 4.1 %while.1 = (s32[]{:T(128)}, f32[256,256]{1,0:T(8,128)S(1)}, s32[2,2]{1,0:T(2,128)S(1)}, f32[2,128,128]{2,1,0:T(8,128)S(1)}, s32[]{:T(128)}) while((s32[]{:T(128)}, f32[256,256]{1,0:T(8,128)S(1)}, s32[2,2]{1,0:T(2,128)S(1)}, f32[2,128,128]{2,1,0:T(8,128)S(1)}, s32[]{:T(128)}) %tuple.29), condition=%wide.while_cond, body=%wide.while_body.sunk | while | flops 2 | bytes 131189 | solution.py:18
  188.2 0.6 fusion.22
  188.8 1.4 bitcast_dynamic-update-slice_fusion.2
  190.2 0.6 fusion.22
  190.8 1.4 bitcast_dynamic-update-slice_fusion.2
  192.3 19.7 %custom-call.16 = f32[2,128,128]{1,2,0:T(8,128)S(1)} custom-call(f32[2,128,128]{2,1,0:T(8,128)S(1)} %get-tuple-element.9), custom_call_target="InvertDiagBlocksLowerTriangular" | custom-call | tf_op jit(solution)/shard_map/jit(_solve_triangular)/triangular_solve | solution.py:18
  212.0 0.4 fusion
  212.4 0.6 convolution_subtract_fusion
  213.0 0.4 fusion.6
  213.5 1.0 copy.6
  214.5 0.8 copy.7
  (10 shorter events, 0.2 us)
Async XLA Ops:
  7.2 1.2 copy-start
  7.2 28.2 %all-reduce.4.cloned.1.call-start = ((), (), s32[]{:S(2)}) async-start(), calls=%async_computation | async-start | bytes 2097152 | tf_op jit(solution)/shard_map/psum | solution.py:12
  12.9 137.0 %all-reduce.6.cloned.1.call-start = ((), (), s32[]{:S(2)}) async-start(), calls=%async_computation.1 | async-start | bytes 524288 | tf_op jit(solution)/shard_map/psum | solution.py:14
Sparse Core Ops, SparseCore 0:
  13.0 22.2 all-reduce.3
  42.0 107.8 all-reduce.5
where the time goes:
time: 223 us; the launch traced here: 222 us
  waiting for transfers between devices  132 us (59%)
  other arithmetic  55.9 us (25%)
  between operations  15.5 us (7%)
  matrix products  10.4 us (5%)
  local copies, waits for them, and re-layouts  8.38 us (4%)
    psum x1, waiting for transfers between devices, local(): gram = lax.psum(local_gram, 'row') / total_rows  109 us
    another operation x6, other arithmetic, local(): factor = jnp.linalg.cholesky(gram).T  34.2 us
    psum x1, waiting for transfers between devices, local(): whole = lax.psum(partial_value, 'col')  22.4 us
    another operation x2, other arithmetic, local(): basis = jax.scipy.linalg.solve_triangular(factor.T, block.T, lower=True).T  19.7 us
    dot_general x1, matrix products, local(): partial_value = jnp.dot(panel, sketch, preferred_element_type=jnp.float32)  4.47 us
  transfers between devices with their start and end apart: 2, of which 2 were waited for; matrix products, arithmetic and copies ran while one was open for 0% of the time, Pallas kernels for 0%

commit v1 on v0

v1 whole, which is shorter than its diff:
```python
import functools

import jax
import jax.numpy as jnp
from jax import lax
from jax.experimental import pallas as pl
from jax.experimental.pallas import tpu as pltpu
from jax.sharding import PartitionSpec as P

MESH = pl.DeviceIdType.MESH
HIGHEST = lax.Precision.HIGHEST
MIB = 1 << 20
LANES = 128
SUB = 8
PANEL = 32
CHUNKS = 4


def radices(count):
    out = []
    while count > 1:
        for r in (4, 2, 3, 5, 7):
            if count % r == 0:
                break
        else:
            r = count
        out.append(r)
        count //= r
    return out


def plan(nrow, height):
    phases, stride = [], 1
    for r in radices(nrow):
        scatter = height % (SUB * r) == 0
        height = height // r if scatter else height
        phases.append((r, stride, height, scatter))
        stride *= r
    return phases


def tdot(a, b):
    return lax.dot_general(a, b, (((0,), (0,)), ((), ())), precision=HIGHEST, preferred_element_type=jnp.float32)


def sample_kernel(nrow, ncol, phases, total_rows, panel, sketch, block, gram, *scratch):
    (pan, sk, psend, precv, gsend, grecv, load_sem, sk_sem, ps_sem, pr_sem, gs_sem, gr_sem, ags_sem, agr_sem), rest = scratch[:14], scratch[14:]
    row, col = lax.axis_index("row"), lax.axis_index("col")
    share, size = block.shape
    height = size // ncol
    step = share // CHUNKS

    copy_sketch = pltpu.make_async_copy(sketch, sk, sk_sem)
    copy_sketch.start()
    loads = {}
    for d in list(range(1, ncol)) + [0]:
        owner = lax.rem(col + d, ncol)
        for c in range(CHUNKS):
            at = pl.ds(pl.multiple_of(owner * share + c * step, step), step)
            loads[d, c] = pltpu.make_async_copy(panel.at[at, :], pan.at[pl.ds((d * CHUNKS + c) * step, step), :], load_sem.at[d * CHUNKS + c])
            loads[d, c].start()

    barrier = pltpu.get_barrier_semaphore()
    count = 0
    for d in range(1, ncol):
        pl.semaphore_signal(barrier, inc=1, device_id=(row, lax.rem(col + d, ncol)), device_id_type=MESH)
        count += 1
    peers = []
    for r, stride, _, _ in phases:
        digit = lax.rem(row // stride, r)
        mine = []
        for d in range(1, r):
            other = lax.rem(digit + d, r)
            target = (row + (other - digit) * stride, col)
            mine.append((other, target))
            pl.semaphore_signal(barrier, inc=1, device_id=target, device_id_type=MESH)
            count += 1
        peers.append((digit, mine))

    sends, arrivals = [], []
    copy_sketch.wait()
    first = True
    for d in range(1, ncol):
        owner = lax.rem(col + d, ncol)
        for c in range(CHUNKS):
            loads[d, c].wait()
            at = pl.ds((d - 1) * share + c * step, step)
            psend[at, :] = jnp.dot(pan[pl.ds((d * CHUNKS + c) * step, step), :], sk[...], preferred_element_type=jnp.float32)
            if first:
                pl.semaphore_wait(barrier, count)
                first = False
            k = (d - 1) * CHUNKS + c
            copy = pltpu.make_async_remote_copy(psend.at[at, :], precv.at[at, :], ps_sem.at[k], pr_sem.at[k], device_id=(row, owner), device_id_type=MESH)
            copy.start()
            sends.append(copy)
            arrivals.append((copy, at, c))
    for c in range(CHUNKS):
        loads[0, c].wait()
        block[pl.ds(c * step, step), :] = jnp.dot(pan[pl.ds(c * step, step), :], sk[...], preferred_element_type=jnp.float32)
    for copy, at, c in arrivals:
        copy.wait_recv()
        own = pl.ds(c * step, step)
        block[own, :] = block[own, :] + precv[at, :]

    arrivals = []
    for d in range(1, ncol):
        owner = lax.rem(col + d, ncol)
        cols = pl.ds(pl.multiple_of(owner * height, height), height)
        gsend[d - 1] = tdot(block[:, cols], block[...])
        copy = pltpu.make_async_remote_copy(gsend.at[d - 1], grecv.at[d - 1], gs_sem.at[d - 1], gr_sem.at[d - 1], device_id=(row, owner), device_id_type=MESH)
        copy.start()
        sends.append(copy)
        arrivals.append(copy)
    cols = pl.ds(pl.multiple_of(col * height, height), height)
    value = tdot(block[:, cols], block[...])
    for d, copy in enumerate(arrivals):
        copy.wait_recv()
        value = value + grecv[d]

    base = col * height
    bases = []
    for i, (r, stride, rows, scatter) in enumerate(phases):
        acc, buf, s_sem, r_sem = rest[4 * i : 4 * i + 4]
        digit, mine = peers[i]
        acc[...] = value
        arrivals = []
        for d, (other, target) in enumerate(mine):
            if scatter:
                src, dst = acc.at[pl.ds(pl.multiple_of(other * rows, rows), rows), :], buf.at[d]
            else:
                src, dst = acc, buf.at[digit]
            copy = pltpu.make_async_remote_copy(src, dst, s_sem.at[d], r_sem.at[d], device_id=target, device_id_type=MESH)
            copy.start()
            sends.append(copy)
            arrivals.append(copy)
        if scatter:
            base = base + digit * rows
            value = acc[pl.ds(pl.multiple_of(digit * rows, rows), rows), :]
            for d, copy in enumerate(arrivals):
                copy.wait_recv()
                value = value + buf[d]
        else:
            buf[digit] = acc[...]
            for copy in arrivals:
                copy.wait_recv()
            value = buf[0]
            for d in range(1, r):
                value = value + buf[d]
        bases.append(base)
    rows = phases[-1][2] if phases else height
    gram[pl.ds(pl.multiple_of(base, rows), rows), :] = value / total_rows

    for i in reversed(range(len(phases))):
        r, stride, rows, scatter = phases[i]
        if not scatter:
            continue
        s_sem, r_sem = rest[4 * i + 2 : 4 * i + 4]
        digit, mine = peers[i]
        at = pl.ds(pl.multiple_of(bases[i], rows), rows)
        arrivals = []
        for d, (other, target) in enumerate(mine):
            copy = pltpu.make_async_remote_copy(gram.at[at, :], gram.at[at, :], s_sem.at[r - 1 + d], r_sem.at[r - 1 + d], device_id=target, device_id_type=MESH)
            copy.start()
            sends.append(copy)
            arrivals.append(copy)
        for copy in arrivals:
            copy.wait_recv()
    arrivals = []
    at = pl.ds(pl.multiple_of(col * height, height), height)
    for d in range(1, ncol):
        copy = pltpu.make_async_remote_copy(gram.at[at, :], gram.at[at, :], ags_sem.at[d - 1], agr_sem.at[d - 1], device_id=(row, lax.rem(col + d, ncol)), device_id_type=MESH)
        copy.start()
        sends.append(copy)
        arrivals.append(copy)
    for copy in arrivals:
        copy.wait_recv()
    for copy in sends:
        copy.wait_send()


def spread(x, at):
    return jnp.broadcast_to(x[at : at + 1, :], x.shape)


def split(x):
    hi = x.astype(jnp.bfloat16)
    left = x - hi.astype(jnp.float32)
    mid = left.astype(jnp.bfloat16)
    return hi, mid, (left - mid.astype(jnp.float32)).astype(jnp.bfloat16)


def recip(d):
    r = pl.reciprocal(d, approx=True)
    r = r * (2.0 - d * r)
    return r * (2.0 - d * r)


def factor_kernel(gram, block, basis, upper, work, inverse):
    size = gram.shape[0]
    tiles = size // LANES
    groups = PANEL // SUB
    sub = lax.broadcasted_iota(jnp.int32, (SUB, LANES), 0)
    lane = lax.broadcasted_iota(jnp.int32, (SUB, LANES), 1)
    work[...] = gram[...]
    rows_of = lax.broadcasted_iota(jnp.int32, (size, size), 0)
    cols_of = lax.broadcasted_iota(jnp.int32, (size, size), 1)
    inverse[...] = jnp.where(rows_of == cols_of, 1.0, 0.0)
    upper[...] = jnp.zeros_like(upper)
    for low in range(0, size, PANEL):
        first = low // LANES
        kinds = [(work, t) for t in range(first, tiles)] + [(inverse, t) for t in range(first + 1)]
        part = [[ref[low + SUB * g : low + SUB * (g + 1), LANES * t : LANES * (t + 1)] for ref, t in kinds] for g in range(groups)]
        off = low % LANES
        column = {}
        for q in range(PANEL):
            for g in range(q // SUB, groups):
                column[q, g] = jnp.broadcast_to(part[g][0][:, off + q : off + q + 1], (SUB, LANES))
        diagonal = [jnp.ones((SUB, LANES), jnp.float32) for _ in range(groups)]
        for p in range(PANEL):
            gp, sp = divmod(p, SUB)
            pivot = spread(column[p, gp], sp)
            diagonal[gp] = jnp.where(sub == sp, pivot, diagonal[gp])
            inv = recip(pivot)
            weight = {g: column[p, g] * inv for g in range(gp, groups)}
            for q in range(p + 1, PANEL):
                value = spread(column[p, q // SUB], q % SUB)
                for g in range(q // SUB, groups):
                    column[q, g] = column[q, g] - weight[g] * value
            weight[gp] = jnp.where(sub > sp, weight[gp], 0.0)
            for x in range(len(kinds)):
                value = spread(part[gp][x], sp)
                for g in range(gp, groups):
                    part[g][x] = part[g][x] - weight[g] * value
        for g in range(groups):
            scale = lax.rsqrt(diagonal[g])
            at = slice(low + SUB * g, low + SUB * (g + 1))
            for x, (ref, t) in enumerate(kinds):
                part[g][x] = part[g][x] * scale
                where = slice(LANES * t, LANES * (t + 1))
                if ref is work:
                    upper[at, where] = jnp.where(lane + LANES * t >= sub + (low + SUB * g), part[g][x], 0.0)
                else:
                    inverse[at, where] = part[g][x]
        if low + PANEL < size:
            wide = (tiles - first) * LANES
            rows = jnp.concatenate([jnp.concatenate(part[g], axis=1) for g in range(groups)], axis=0)
            hi, mid, lo = split(rows)
            left = jnp.concatenate([x[:, :wide] for x in (hi, hi, mid, hi, lo, mid)], axis=0)
            right = jnp.concatenate([hi, mid, hi, lo, hi, mid], axis=0)
            change = lax.dot_general(left, right, (((0,), (0,)), ((), ())), preferred_element_type=jnp.float32)
            skip = low + PANEL - first * LANES
            work[low + PANEL :, first * LANES :] = work[low + PANEL :, first * LANES :] - change[skip:, :wide]
            inverse[low + PANEL :, : (first + 1) * LANES] = inverse[low + PANEL :, : (first + 1) * LANES] - change[skip:, wide:]
    basis[...] = lax.dot_general(block[...], inverse[...], (((1,), (1,)), ((), ())), precision=HIGHEST, preferred_element_type=jnp.float32)


def local(panel, sketch):
    rows, depth = panel.shape
    size = sketch.shape[1]
    ncol, nrow = lax.axis_size("col"), lax.axis_size("row")
    share, height = rows // ncol, size // ncol
    phases = plan(nrow, height)
    f32 = jnp.float32
    dma = pltpu.SemaphoreType.DMA
    vmem = pl.BlockSpec(memory_space=pltpu.VMEM)
    anywhere = pl.BlockSpec(memory_space=pl.ANY)
    others = max(ncol - 1, 1)
    scratch = [
        pltpu.VMEM((rows, depth), panel.dtype),
        pltpu.VMEM((depth, size), sketch.dtype),
        pltpu.VMEM((others * share, size), f32),
        pltpu.VMEM((others * share, size), f32),
        pltpu.VMEM((others, height, size), f32),
        pltpu.VMEM((others, height, size), f32),
        dma((ncol * CHUNKS,)),
        dma,
        dma((others * CHUNKS,)),
        dma((others * CHUNKS,)),
        dma((others,)),
        dma((others,)),
        dma((others,)),
        dma((others,)),
    ]
    tall = height
    for r, _, piece, scatter in phases:
        scratch += [
            pltpu.VMEM((tall, size), f32),
            pltpu.VMEM((r - 1 if scatter else r, piece, size), f32),
            dma((2 * (r - 1),)),
            dma((2 * (r - 1),)),
        ]
        tall = piece
    block, gram = pl.pallas_call(
        functools.partial(sample_kernel, nrow, ncol, phases, float(rows * nrow)),
        out_shape=(jax.ShapeDtypeStruct((share, size), f32), jax.ShapeDtypeStruct((size, size), f32)),
        in_specs=[anywhere, anywhere],
        out_specs=(vmem, vmem),
        scratch_shapes=scratch,
        compiler_params=pltpu.CompilerParams(collective_id=0, has_side_effects=True, vmem_limit_bytes=32 * MIB),
        cost_estimate=pl.CostEstimate(flops=2 * rows * depth * size, bytes_accessed=2 * (rows + size) * depth, transcendentals=0),
        name="sample",
    )(panel, sketch)
    return pl.pallas_call(
        factor_kernel,
        out_shape=(jax.ShapeDtypeStruct((share, size), f32), jax.ShapeDtypeStruct((size, size), f32)),
        in_specs=[vmem, vmem],
        out_specs=(vmem, vmem),
        scratch_shapes=[pltpu.VMEM((size, size), f32), pltpu.VMEM((size, size), f32)],
        compiler_params=pltpu.CompilerParams(vmem_limit_bytes=32 * MIB),
        cost_estimate=pl.CostEstimate(flops=2 * share * size * size, bytes_accessed=8 * (share + size) * size, transcendentals=0),
        name="factor",
    )(gram, block)


def solution(mesh):
    return jax.shard_map(
        local,
        mesh=mesh,
        in_specs=(P("row", "col"), P("col", None)),
        out_specs=(P(("row", "col"), None), P()),
        check_vma=False,
    )
```

time: 223 us -> 40 us (0.18)
  waiting for transfers between devices: 132 us -> 0 us
  other arithmetic: 55.9 us -> 0 us
  Pallas kernels: 0 us -> 35.7 us
  between operations: 15.5 us -> 0.65 us
  matrix products: 10.4 us -> 0 us
  local copies, waits for them, and re-layouts: 8.38 us -> 3.41 us
    psum x2 -> x0, waiting for transfers between devices: 132 us -> none  [the longest x1 109 us: local(): gram = lax.psum(local_gram, 'row') / total_rows]
    another operation x8 -> x0, other arithmetic: 53.9 us -> none  [the longest x6 34.2 us: local(): factor = jnp.linalg.cholesky(gram).T]
    pallas_call x0 -> x2, Pallas kernels: none -> 35.7 us  [the longest x1 26.8 us: local(): pl.pallas_call(functools.partial(sample_kernel, nrow, ncol, phases, float...]
    dot_general x2 -> x0, matrix products: 8.54 us -> none  [the longest x1 4.47 us: local(): partial_value = jnp.dot(panel, sketch, preferred_element_type=jnp.float32)]
    another operation x9 -> x0, local copies, waits for them, and re-layouts: 4.16 us -> none
  transfers between devices with their start and end apart: 2 -> 0, of which waited for: 2 -> 0; matrix products, arithmetic and copies ran while one was open for 0% -> 0% of each run, Pallas kernels for 0% -> 0%
where the time goes in v1:
time: 40 us; the launch traced here: 39.8 us
  Pallas kernels  35.7 us (89%)
  local copies, waits for them, and re-layouts  3.41 us (9%)
  between operations  0.65 us (2%)
    pallas_call x1, Pallas kernels, local(): pl.pallas_call(functools.partial(sample_kernel, nrow, ncol, phases, float...  26.8 us
    pallas_call x1, Pallas kernels, local(): pl.pallas_call(factor_kernel, out_shape=(jax.ShapeDtypeStruct((share, siz...  8.98 us
    unnamed x4, local copies, waits for them, and re-layouts  3.41 us

profile of v1, /device:TPU:0, one launch (start us, length us, event | category | flops | bytes accessed | tf_op | source)
XLA Modules:
  0.0 39.8 jit_solution(12065253018431688001)
XLA Ops:
  0.6 0.0 copy-start
  0.6 2.2 %copy-done = bf16[1024,2048]{1,0:T(8,128)(2,1)S(1)} copy-done((bf16[1024,2048]{1,0:T(8,128)(2,1)S(1)}, bf16[1024,2048]{1,0:T(8,128)(2,1)}, u32[]{:S(2)}) %copy-start) | copy-done | bytes 4194328
  2.8 0.0 copy-start.1
  2.8 1.2 %copy-done.1 = bf16[2048,256]{1,0:T(8,128)(2,1)S(1)} copy-done((bf16[2048,256]{1,0:T(8,128)(2,1)S(1)}, bf16[2048,256]{1,0:T(8,128)(2,1)}, u32[]{:S(2)}) %copy-start.1) | copy-done | bytes 1048600
  4.0 26.8 %sample.1 = (f32[512,256]{1,0:T(8,128)S(1)}, f32[256,256]{1,0:T(8,128)S(1)}) custom-call(bf16[1024,2048]{1,0:T(8,128)(2,1)S(1)} %copy-done, bf16[2048,256]{1,0:T(8,128)(2,1)S(1)} %copy-done.1), custom_call_target="tpu_custom_call" | custom-call | flops 1073741824 | bytes 5242880 | tf_op jit(solution)/shard_map/sample/pallas_call | solution.py:293
  30.8 9.0 %factor.1 = (f32[512,256]{1,0:T(8,128)}, f32[256,256]{1,0:T(8,128)}) custom-call(f32[256,256]{1,0:T(8,128)S(1)} %get-tuple-element.4.gram, f32[512,256]{1,0:T(8,128)S(1)} %get-tuple-element.5.block), custom_call_target="tpu_custom_call" | custom-call | flops 67108864 | bytes 1572864 | tf_op jit(solution)/shard_map/factor/pallas_call | solution.py:303
Async XLA Ops:
  0.6 2.2 %copy-start = (bf16[1024,2048]{1,0:T(8,128)(2,1)S(1)}, bf16[1024,2048]{1,0:T(8,128)(2,1)}, u32[]{:S(2)}) copy-start(bf16[1024,2048]{1,0:T(8,128)(2,1)} %panel.1) | copy-start | bytes 12582916
  2.8 1.2 %copy-start.1 = (bf16[2048,256]{1,0:T(8,128)(2,1)S(1)}, bf16[2048,256]{1,0:T(8,128)(2,1)}, u32[]{:S(2)}) copy-start(bf16[2048,256]{1,0:T(8,128)(2,1)} %sketch.1) | copy-start | bytes 3145732
